TPU v7x, 256 devices: a whole 4x4x8 slice. The times are simulated.
256 devices in a mesh: row: 16 (over x_lo, z), col: 4 (over y), ka: 4 (over x_hi, core).
Axes of the slice: x: 4 (x_hi: 2, x_lo: 2; x = x_hi * 2 + x_lo), y: 4, z: 8, core: 2. Of those that a mesh axis runs over, the one named last changes fastest.
Arguments:
- pair: bfloat16 [1024, 1024, 128], P('row', ('col', 'ka')), may hold values from -6 to 6
- in_gain: float32 [128], replicated, may hold values from 0.25 to 1.75
- in_shift: float32 [128], replicated, may hold values from -0.45 to 0.45
- w_inner: bfloat16 [128, 512], replicated, may hold values from -0.5 to 0.5
- inner_bias: float32 [512], replicated, may hold values from -3 to 3
- gate_weight: bfloat16 [128, 128], replicated, may hold values from -0.5 to 0.5
- gate_bias: float32 [128], replicated, may hold values from -3 to 3
- out_gain: float32 [128], replicated, may hold values from 0.25 to 1.75
- out_shift: float32 [128], replicated, may hold values from -3 to 3
- out_weight: bfloat16 [128, 128], replicated, may hold values from -0.5 to 0.5
- out_bias: float32 [128], replicated, may hold values from -3 to 3
Outputs:
- update: bfloat16 [1024, 1024, 128], P('row', ('col', 'ka'))
All inputs are finite; a program needn't handle non-finite values.
Results may differ from a plain program's by a relative error of at most 0.014.
Values may be sent and summed in bfloat16 or wider, within the bound.
A program may use at most 192 MiB of HBM per device.

v0:
```python
import jax
import jax.numpy as jnp
from jax import lax
from jax.sharding import PartitionSpec as P


def layer_norm(values, gain, shift):
    mean = jnp.mean(values, axis=-1, keepdims=True)
    centred = values - mean
    variance = jnp.mean(centred * centred, axis=-1, keepdims=True)
    return centred * lax.rsqrt(variance + 1e-05) * gain + shift


def on_device(
    pair,
    in_gain,
    in_shift,
    w_inner,
    inner_bias,
    gate_weight,
    gate_bias,
    out_gain,
    out_shift,
    out_weight,
    out_bias,
):
    row_count, col_count, width = pair.shape
    hidden = out_weight.shape[0]
    normed = layer_norm(pair.astype(jnp.float32), in_gain, in_shift).astype(jnp.bfloat16)
    flat = normed.reshape(row_count * col_count, width)
    inner = jnp.dot(flat, w_inner, preferred_element_type=jnp.float32) + inner_bias
    left = (jax.nn.sigmoid(inner[:, hidden : 2 * hidden]) * inner[:, :hidden]).astype(jnp.bfloat16)
    right = (jax.nn.sigmoid(inner[:, 3 * hidden :]) * inner[:, 2 * hidden : 3 * hidden]).astype(
        jnp.bfloat16
    )
    gate = jax.nn.sigmoid(
        jnp.dot(flat, gate_weight, preferred_element_type=jnp.float32) + gate_bias
    )
    left = left.reshape(row_count, col_count, hidden)
    right = right.reshape(row_count, col_count, hidden)
    terms = jnp.einsum(
        "ikh,jkh->ijh",
        left,
        lax.all_gather(right, "row", axis=0, tiled=True),
        preferred_element_type=jnp.float32,
    )
    tri = lax.psum_scatter(terms, ("col", "ka"), scatter_dimension=1, tiled=True).astype(
        jnp.bfloat16
    )
    tri_normed = layer_norm(tri.astype(jnp.float32), out_gain, out_shift).astype(jnp.bfloat16)
    projected = jnp.dot(
        tri_normed.reshape(row_count * col_count, hidden),
        out_weight,
        preferred_element_type=jnp.float32,
    )
    update = gate * (projected + out_bias)
    return update.reshape(row_count, col_count, width).astype(jnp.bfloat16)


def solution(mesh):
    placed = (P("row", ("col", "ka"), None), P(), P(), P(), P(), P(), P(), P(), P(), P(), P())
    return jax.shard_map(
        on_device,
        mesh=mesh,
        in_specs=placed,
        out_specs=P("row", ("col", "ka"), None),
        check_vma=False,
    )
```

profile of v0, /device:TPU:6, one launch (start us, length us, event | category | flops | bytes accessed | tf_op | source)
XLA Modules:
  0.0 704.1 jit_solution(13624831825121763622)
XLA Ops:
  6.5 0.0 copy-start
  6.5 0.0 copy-start.3
  6.5 0.0 copy-start.10
  6.5 0.0 copy-start.9
  6.5 0.0 copy-start.5
  6.5 0.0 all-gather.2.cloned.1.call-start
  6.6 1.9 convert_reduce_fusion.1
  8.5 2.3 fusion.14
  10.9 0.0 copy-done.3
  10.9 0.0 copy-done.10
  10.9 0.0 copy-done.9
  10.9 1.3 fusion.17
  12.2 0.0 copy-done
  12.2 0.0 copy-done.5
  12.2 1.2 convolution_add_fusion
  13.5 2.1 fusion.18
  15.5 3.8 copy.17
  19.3 0.0 all-gather.2.cloned.1.call-update
  19.3 0.2 reduce-scatter.2.cloned.1.call-start
  19.5 3.9 copy.18
  23.5 352.0 %all-gather.2.cloned.1.call-done = bf16[1024,64,128]{1,0,2:T(8,128)(2,1)} async-done(((bf16[64,64,128]{1,0,2:T(8,128)(2,1)}), bf16[1024,64,128]{1,0,2:T(8,128)(2,1)}) %all-gather.2.cloned.1.call-update) | async-done | bytes 16777232 | tf_op jit(solution)/shard_map/all_gather | solution.py:44
  375.5 24.8 %convolution_bitcast_fusion = f32[64,1024,128]{1,0,2:T(8,128)} fusion(bf16[1024,64,128]{1,0,2:T(8,128)(2,1)} %all-gather.2.cloned.1.call-done, bf16[64,64,128]{1,0,2:T(8,128)(2,1)S(1)} %copy.18), kind=kOutput, calls=%fused_computation | convolution fusion | flops 1073741824 | bytes 51380224 | tf_op jit(solution)/shard_map/ikh,jkh->ijh/dot_general | solution.py:41
  400.3 32.6 %copy.19 = f32[64,1024,128]{2,0,1:T(8,128)} copy(f32[64,1024,128]{1,0,2:T(8,128)} %convolution_bitcast_fusion) | data formatting | bytes 67108864 | tf_op jit(solution)/shard_map/ikh,jkh->ijh/transpose | solution.py:41
  432.9 0.0 copy-start.11
  432.9 0.0 copy-start.12
  432.9 0.0 reduce-scatter.2.cloned.1.call-update
  433.0 0.7 copy-done.11
  433.7 0.0 copy-done.12
  433.7 0.7 fusion.4
  434.4 0.0 copy-start.6
  434.4 0.0 copy-start.7
  434.4 252.0 %reduce-scatter.2.cloned.1.call-done = f32[64,64,128]{2,0,1:T(8,128)} async-done(((f32[64,1024,128]{2,0,1:T(8,128)}), f32[64,64,128]{2,0,1:T(8,128)}) %reduce-scatter.2.cloned.1.call-update) | async-done | bytes 2097168 | tf_op jit(solution)/shard_map/reduce_scatter | solution.py:47
  686.4 0.0 copy-start.2
  686.4 3.4 convert_reduce_fusion
  689.9 0.0 copy-done.2
  689.9 3.2 fusion.10
  693.1 0.0 copy-start.4
  693.1 0.0 copy-start.8
  693.1 0.0 copy-done.6
  693.2 0.0 copy-done.7
  693.2 2.6 fusion.13
  695.8 0.0 copy-start.1
  695.8 0.0 copy-done.4
  695.8 0.0 copy-done.8
  695.9 1.4 fusion.5
  697.2 0.0 copy-done.1
  (4 shorter events, 0.0 us)
Async XLA Ops:
  6.5 5.7 copy-start
  6.5 4.4 copy-start.3
  6.5 4.4 copy-start.10
  6.5 4.4 copy-start.9
  6.5 5.7 copy-start.5
  6.5 369.0 %all-gather.2.cloned.1.call-start = ((), (), s32[]{:S(2)}) async-start(), calls=%async_computation.1 | async-start | bytes 35651584 | tf_op jit(solution)/shard_map/all_gather | solution.py:44
  19.3 667.1 %reduce-scatter.2.cloned.1.call-start = ((), (), s32[]{:S(2)}) async-start(), calls=%async_computation.2 | async-start | bytes 35651584 | tf_op jit(solution)/shard_map/reduce_scatter | solution.py:47
  432.9 0.8 copy-start.11
  432.9 0.8 copy-start.12
  434.4 258.8 %copy-start.6 = (f32[128]{0:T(128)S(1)}, f32[128]{0:T(128)}, u32[]{:S(2)}) copy-start(f32[128]{0:T(128)} %param.19) | copy-start | bytes 1540
  434.4 258.7 %copy-start.7 = (f32[128]{0:T(128)S(1)}, f32[128]{0:T(128)}, u32[]{:S(2)}) copy-start(f32[128]{0:T(128)} %param.18) | copy-start | bytes 1540
  686.4 3.5 copy-start.2
  693.1 2.7 copy-start.4
  693.1 2.7 copy-start.8
  695.8 1.4 copy-start.1
Sparse Core Ops, SparseCore 0:
  19.4 356.0 all-gather.1
  433.1 253.2 reduce-scatter.1
where the time goes:
time: 705 us; the launch traced here: 704 us
  waiting for transfers between devices  604 us (86%)
  local copies, waits for them, and re-layouts  41.1 us (6%)
  matrix products  28.1 us (4%)
  other arithmetic  16.9 us (2%)
  between operations  13.6 us (2%)
    all_gather x1, waiting for transfers between devices, on_device(): lax.all_gather(right, 'row', axis=0, tiled=True)  352 us
    reduce_scatter x1, waiting for transfers between devices, on_device(): lax.psum_scatter(terms, ('col', 'ka'), scatter_dimension=1, tiled=True)  252 us
    transpose x1, local copies, waits for them, and re-layouts, on_device(): jnp.einsum('ikh,jkh->ijh', left, lax.all_gather(right, 'row', axis=0, til...  32.6 us
    dot_general x1, matrix products, on_device(): jnp.einsum('ikh,jkh->ijh', left, lax.all_gather(right, 'row', axis=0, til...  24.8 us
  transfers between devices with their start and end apart: 2, of which 2 were waited for; matrix products, arithmetic and copies ran while one was open for 1% of the time, Pallas kernels for 0%

commit v1 on v0

v1 whole, which is shorter than its diff:
```python
import functools

import jax
import jax.numpy as jnp
from jax import lax
from jax.experimental import pallas as pl
from jax.experimental.pallas import tpu as pltpu
from jax.sharding import PartitionSpec as P

MESH = pl.DeviceIdType.MESH
CHIPS = 128
ROWS = 16
BF16, F32 = jnp.bfloat16, jnp.float32
NT = (((1,), (1,)), ((), ()))


def sigmoid(x):
    return 0.5 * jnp.tanh(0.5 * x) + 0.5


def normalise(x, gain, shift):
    mean = jnp.sum(x, axis=0, keepdims=True) * (1.0 / 128)
    centred = x - mean
    variance = jnp.sum(centred * centred, axis=0, keepdims=True) * (1.0 / 128)
    return centred * lax.rsqrt(variance + 1e-05) * gain + shift


def twice(column):
    return jnp.concatenate([column, column], axis=1)


def kernel(
    pair, in_gain, in_shift, w_inner, inner_bias, gate_weight, gate_bias, out_gain, out_shift, out_weight, out_bias,
    out,
    cols, w_t, gw_t, ow_t, flat, normed, send1, recv1, left_m, right_m, acc, part_out, part_in, send2, recv2, gate,
    send1_sem, recv1_sem, part_send_sem, part_recv_sem, send2_sem, recv2_sem,
):
    row, col, ka = lax.axis_index("row"), lax.axis_index("col"), lax.axis_index("ka")
    core = lax.rem(ka, 2)
    x, z = (ka // 2) * 2 + row // 8, lax.rem(row, 8)
    me = (col * 2 + ka // 2) * ROWS + row

    def partner(step):
        tz = lax.rem(z + step % 8, 8)
        tx = lax.rem(x + (step // 8) % 4, 4)
        ty = lax.rem(col + step // 32, 4)
        trow = lax.rem(tx, 2) * 8 + tz
        return (ty * 2 + tx // 2) * ROWS + trow, (trow, ty, (tx // 2) * 2 + core)

    sibling = (row, col, (ka // 2) * 2 + 1 - core)

    barrier = pltpu.get_barrier_semaphore()

    def greet(step, _):
        pl.semaphore_signal(barrier, inc=1, device_id=partner(step)[1], device_id_type=MESH)
        return 0

    lax.fori_loop(1, CHIPS, greet, 0)
    pl.semaphore_signal(barrier, inc=1, device_id=sibling, device_id_type=MESH)

    rows = [in_gain[...], in_shift[...]]
    rows += [inner_bias[:, 128 * i : 128 * i + 128] for i in range(4)]
    rows += [gate_bias[...], out_gain[...], out_shift[...], out_bias[...]]
    for i, values in enumerate(rows):
        cols[i] = jnp.broadcast_to(values, (128, 128)).T
    w_t[...] = w_inner[...].astype(F32).T.astype(BF16)
    gw_t[...] = gate_weight[...].astype(F32).T.astype(BF16)
    ow_t[...] = out_weight[...].astype(F32).T.astype(BF16)

    def project(r, _):
        r0 = 2 * r
        block = jnp.concatenate([pair[r0], pair[r0 + 32], pair[r0 + 1], pair[r0 + 33]], axis=0)
        n = normalise(block.astype(F32).T, twice(cols[0]), twice(cols[1])).astype(BF16)
        normed[r] = n
        inner = jnp.dot(w_t[...], n, preferred_element_type=F32)
        left = sigmoid(inner[128:256] + twice(cols[3])) * (inner[:128] + twice(cols[2]))
        right = sigmoid(inner[384:] + twice(cols[5])) * (inner[256:384] + twice(cols[4]))
        for half in range(2):
            at = pl.multiple_of((r0 + half) * 256, 256)
            flat[pl.ds(at, 128), :] = left[:, half * 128 : half * 128 + 128]
            flat[pl.ds(at + 128, 128), :] = right[:, half * 128 : half * 128 + 128]
        return 0

    lax.fori_loop(0, 16, project, 0)
    pl.semaphore_wait(barrier, CHIPS)

    def channel(h):
        l = flat[pl.ds(h, 32, stride=256), :]
        r = flat[pl.ds(h + 128, 32, stride=256), :]
        return jnp.concatenate([l, r], axis=0).astype(BF16)

    def scatter(step, _):
        chip, device = partner(step)
        send1[chip] = channel(chip)
        pltpu.make_async_remote_copy(
            send1.at[chip], recv1.at[me], send1_sem, recv1_sem, device_id=device, device_id_type=MESH
        ).start()
        return 0

    lax.fori_loop(1, CHIPS, scatter, 0)
    recv1[me] = channel(me)

    def gates(r, _):
        g = jnp.dot(gw_t[...], normed[r], preferred_element_type=F32) + twice(cols[6])
        gate[r] = sigmoid(g)
        return 0

    lax.fori_loop(0, 16, gates, 0)

    others = pl.ds(0, CHIPS - 1)
    pltpu.make_async_copy(recv1.at[others], recv1.at[others], recv1_sem).wait()

    def assemble(b, _):
        at_l = pl.multiple_of(lax.rem(b, 4) * 256 + (b // 8) * 128 + (lax.rem(b, 8) // 4) * 64, 64)
        at_r = pl.multiple_of(lax.rem(b, 2) * 512 + (b // 2) * 64, 64)
        for p in range(4):
            one, two = recv1[2 * p * ROWS + b], recv1[(2 * p + 1) * ROWS + b]
            low = jnp.concatenate([one[:, :64], two[:, :64]], axis=1)
            high = jnp.concatenate([one[:, 64:], two[:, 64:]], axis=1)
            k = slice(p * 128, p * 128 + 128)
            left_m[pl.ds(at_l, 32), k] = low[:32]
            left_m[pl.ds(at_l + 32, 32), k] = high[:32]
            right_m[pl.ds(at_r, 32), k] = low[32:]
            right_m[pl.ds(at_r + 32, 32), k] = high[32:]
        return 0

    lax.fori_loop(0, ROWS, assemble, 0)

    def group(i):
        return lax.rem(lax.rem(z, 4) + i, 4)

    def part_copy(g):
        return pltpu.make_async_remote_copy(
            part_out.at[g], part_in.at[g], part_send_sem.at[g], part_recv_sem.at[g],
            device_id=sibling, device_id_type=MESH,
        )

    def block_product(g, half):
        lhs = left_m[pl.ds(pl.multiple_of(g * 256, 256), 256), :]
        rhs = right_m[pl.ds(pl.multiple_of(half * 512, 512), 512), :]
        return lax.dot_general(lhs, rhs, NT, preferred_element_type=F32)

    def multiply_other(i, _):
        g = group(i)
        part_out[g] = block_product(g, 1 - core).astype(BF16)
        part_copy(g).start()
        return 0

    def multiply_own(i, _):
        acc[group(i)] = block_product(group(i), core)
        return 0

    lax.fori_loop(0, 4, multiply_other, 0)
    lax.fori_loop(0, 4, multiply_own, 0)

    def give_back(i, _):
        g = group(i)
        part_copy(g).wait_recv()

        def per_row(j, _):
            at = pl.ds(pl.multiple_of(j * 64, 64), 64)
            trow = (j // 2) * 8 + lax.rem(j, 2) * 4 + g
            tri = (acc[g, at, :] + part_in[g, at, :].astype(F32)).astype(BF16)
            for kb in range(8):
                tile = jnp.concatenate([tri[:32, kb * 64 : kb * 64 + 64], tri[32:, kb * 64 : kb * 64 + 64]], axis=1)
                chip = kb * ROWS + trow

                @pl.when(chip == me)
                def _():
                    recv2[me] = tile

                @pl.when(chip != me)
                def _():
                    send2[chip] = tile
                    pltpu.make_async_remote_copy(
                        send2.at[chip], recv2.at[me], send2_sem, recv2_sem,
                        device_id=(trow, kb // 2, (kb % 2) * 2 + core), device_id_type=MESH,
                    ).start()

            return 0

        lax.fori_loop(0, 4, per_row, 0)
        return 0

    lax.fori_loop(0, 4, give_back, 0)
    pltpu.make_async_copy(recv2.at[others], recv2.at[others], recv2_sem).wait()

    def widen(h, _):
        flat[pl.ds(pl.multiple_of(h * 32, 32), 32), :] = recv2[h].astype(F32)
        return 0

    lax.fori_loop(0, CHIPS, widen, 0)

    def finish(r, _):
        r0 = 2 * r
        t = jnp.concatenate(
            [flat[pl.ds(r0, 128, stride=32), :], flat[pl.ds(r0 + 1, 128, stride=32), :]], axis=1
        )
        n = normalise(t, twice(cols[7]), twice(cols[8])).astype(BF16)
        projected = jnp.dot(ow_t[...], n, preferred_element_type=F32) + twice(cols[9])
        update = (gate[r] * projected).T.astype(BF16)
        out[r0] = update[:64]
        out[r0 + 32] = update[64:128]
        out[r0 + 1] = update[128:192]
        out[r0 + 33] = update[192:]
        return 0

    lax.fori_loop(0, 16, finish, 0)

    pltpu.make_async_copy(send1.at[others], send1.at[others], send1_sem).wait()
    pltpu.make_async_copy(send2.at[others], send2.at[others], send2_sem).wait()
    for g in range(4):
        part_copy(g).wait_send()


def on_device(pair, in_gain, in_shift, w_inner, inner_bias, gate_weight, gate_bias, out_gain, out_shift, out_weight, out_bias):
    vmem = pl.BlockSpec(memory_space=pltpu.VMEM)
    dma = pltpu.SemaphoreType.DMA
    as_row = lambda v: v.reshape(1, -1)
    return pl.pallas_call(
        kernel,
        out_shape=jax.ShapeDtypeStruct((64, 64, 128), BF16),
        in_specs=[vmem] * 11,
        out_specs=vmem,
        scratch_shapes=[
            pltpu.VMEM((10, 128, 128), F32),
            pltpu.VMEM((512, 128), BF16),
            pltpu.VMEM((128, 128), BF16),
            pltpu.VMEM((128, 128), BF16),
            pltpu.VMEM((32 * 256, 128), F32),
            pltpu.VMEM((16, 128, 256), BF16),
            pltpu.VMEM((CHIPS, 64, 128), BF16),
            pltpu.VMEM((CHIPS, 64, 128), BF16),
            pltpu.VMEM((1024, 512), BF16),
            pltpu.VMEM((1024, 512), BF16),
            pltpu.VMEM((4, 256, 512), F32),
            pltpu.VMEM((4, 256, 512), BF16),
            pltpu.VMEM((4, 256, 512), BF16),
            pltpu.VMEM((CHIPS, 32, 128), BF16),
            pltpu.VMEM((CHIPS, 32, 128), BF16),
            pltpu.VMEM((16, 128, 256), F32),
            dma, dma, dma((4,)), dma((4,)), dma, dma,
        ],
        compiler_params=pltpu.CompilerParams(
            collective_id=0, has_side_effects=True, vmem_limit_bytes=40 * 2**20
        ),
    )(
        pair, as_row(in_gain), as_row(in_shift), w_inner, as_row(inner_bias), gate_weight, as_row(gate_bias),
        as_row(out_gain), as_row(out_shift), out_weight, as_row(out_bias),
    )


def solution(mesh):
    placed = (P("row", ("col", "ka"), None),) + (P(),) * 10
    return jax.shard_map(
        on_device, mesh=mesh, in_specs=placed, out_specs=P("row", ("col", "ka"), None), check_vma=False
    )
```

time: 705 us -> 109 us (0.15)
  waiting for transfers between devices: 604 us -> 0 us
  Pallas kernels: 0 us -> 104 us
  local copies, waits for them, and re-layouts: 41.1 us -> 5.33 us
  matrix products: 28.1 us -> 0 us
  other arithmetic: 16.9 us -> 0 us
  between operations: 13.6 us -> 0.05 us
    all_gather x1 -> x0, waiting for transfers between devices: 352 us -> none  [on_device(): lax.all_gather(right, 'row', axis=0, tiled=True)]
    reduce_scatter x1 -> x0, waiting for transfers between devices: 252 us -> none  [on_device(): lax.psum_scatter(terms, ('col', 'ka'), scatter_dimension=1, tiled=True)]
    pallas_call x0 -> x1, Pallas kernels: none -> 104 us  [on_device(): pl.pallas_call(kernel, out_shape=jax.ShapeDtypeStruct((64, 64, 128), BF16...]
    transpose x1 -> x0, local copies, waits for them, and re-layouts: 32.6 us -> none  [on_device(): jnp.einsum('ikh,jkh->ijh', left, lax.all_gather(right, 'row', axis=0, til...]
    dot_general x4 -> x0, matrix products: 28.1 us -> none  [the longest x1 24.8 us: on_device(): jnp.einsum('ikh,jkh->ijh', left, lax.all_gather(right, 'row', axis=0, til...]
    reduce_sum x4 -> x0, other arithmetic: 10.9 us -> none  [the longest x2 5.54 us: layer_norm(): variance = jnp.mean(centred * centred, axis=-1, keepdims=True)]
    reshape x2 -> x0, local copies, waits for them, and re-layouts: 7.7 us -> none  [the longest x1 3.94 us: on_device(): left = left.reshape(row_count, col_count, hidden)]
  transfers between devices with their start and end apart: 2 -> 0, of which waited for: 2 -> 0; matrix products, arithmetic and copies ran while one was open for 1% -> 0% of each run, Pallas kernels for 0% -> 0%
where the time goes in v1:
time: 109 us
  Pallas kernels  104 us (95%)
  local copies, waits for them, and re-layouts  5.33 us (5%)
    pallas_call x1, Pallas kernels, on_device(): pl.pallas_call(kernel, out_shape=jax.ShapeDtypeStruct((64, 64, 128), BF16...  104 us
    unnamed x23, local copies, waits for them, and re-layouts  5.33 us

profile of v1, /device:TPU:6, one launch (start us, length us, event | category | flops | bytes accessed | tf_op | source)
XLA Modules:
  0.0 109.1 jit_solution(13353856845111151894)
XLA Ops:
  0.0 0.0 copy-start.8
  0.0 0.0 copy-start.9
  0.0 0.0 copy-start.10
  0.0 0.0 copy-start.4
  0.0 0.0 copy-start.5
  0.0 0.0 copy-start.6
  0.0 0.0 copy-start.7
  0.0 0.6 copy-done.8
  0.7 0.0 copy-done.9
  0.7 0.0 copy-done.10
  0.7 0.0 copy-done.4
  0.7 0.0 copy-done.5
  0.7 0.0 copy-done.6
  0.7 0.0 copy-done.7
  0.8 0.0 copy-start
  0.8 1.2 %copy-done = bf16[64,64,128]{2,1,0:T(8,128)(2,1)S(1)} copy-done((bf16[64,64,128]{2,1,0:T(8,128)(2,1)S(1)}, bf16[64,64,128]{2,1,0:T(8,128)(2,1)}, u32[]{:S(2)}) %copy-start) | copy-done | bytes 1048600
  2.0 0.0 copy-start.1
  2.0 0.9 copy-done.1
  2.9 0.0 copy-start.2
  2.9 0.8 copy-done.2
  3.6 0.0 copy-start.3
  3.6 0.8 copy-done.3
  4.4 103.7 %shard_map.109 = bf16[64,64,128]{2,1,0:T(8,128)(2,1)S(1)} custom-call(bf16[64,64,128]{2,1,0:T(8,128)(2,1)S(1)} %copy-done, f32[1,128]{1,0:T(1,128)S(1)} %bitcast.8, f32[1,128]{1,0:T(1,128)S(1)} %bitcast.9, bf16[128,512]{1,0:T(8,128)(2,1)S(1)} %copy-done.1, f32[1,512]{1,0:T(1,128)S(1)} %bitcast.7, bf16[128,128]{1,0:T(8,128)(2,1)S(1)} %copy-done.2, ...), custom_call_target="tpu_custom_call" | custom-call | tf_op jit(solution)/shard_map/pallas_call | solution.py:220
  108.1 1.0 copy.13
Async XLA Ops:
  0.0 0.7 copy-start.8
  0.0 0.7 copy-start.9
  0.0 0.7 copy-start.10
  0.0 0.7 copy-start.4
  0.0 0.7 copy-start.5
  0.0 0.7 copy-start.6
  0.0 0.7 copy-start.7
  0.8 1.2 %copy-start = (bf16[64,64,128]{2,1,0:T(8,128)(2,1)S(1)}, bf16[64,64,128]{2,1,0:T(8,128)(2,1)}, u32[]{:S(2)}) copy-start(bf16[64,64,128]{2,1,0:T(8,128)(2,1)} %pair.1) | copy-start | bytes 3145732
  2.0 0.9 copy-start.1
  2.9 0.8 copy-start.2
  3.6 0.8 copy-start.3

commit v2 on v1

--- a/solution.py
+++ b/solution.py
@@ -11,6 +11,10 @@
 CHIPS = 128
 ROWS = 16
 BF16, F32 = jnp.bfloat16, jnp.float32
+SMALL = [
+    ((1, 128), F32), ((1, 128), F32), ((128, 512), BF16), ((1, 512), F32), ((128, 128), BF16),
+    ((1, 128), F32), ((1, 128), F32), ((1, 128), F32), ((128, 128), BF16), ((1, 128), F32),
+]
 NT = (((1,), (1,)), ((), ()))
 
 
@@ -30,11 +34,26 @@
 
 
 def kernel(
-    pair, in_gain, in_shift, w_inner, inner_bias, gate_weight, gate_bias, out_gain, out_shift, out_weight, out_bias,
-    out,
+    pair_hbm, *refs
+):
+    small_hbm, out_hbm, refs = refs[:10], refs[10], refs[11:]
+    small, refs = refs[:10], refs[10:]
+    in_gain, in_shift, w_inner, inner_bias, gate_weight, gate_bias, out_gain, out_shift, out_weight, out_bias = small
+    (
+    pair, out, small_sem, pair_sem, out_sem, plane_sem, all_sem,
     cols, w_t, gw_t, ow_t, flat, normed, send1, recv1, left_m, right_m, acc, part_out, part_in, send2, recv2, gate,
     send1_sem, recv1_sem, part_send_sem, part_recv_sem, send2_sem, recv2_sem,
-):
+    ) = refs
+    small_copies = [pltpu.make_async_copy(a, b, small_sem.at[i]) for i, (a, b) in enumerate(zip(small_hbm, small))]
+
+    def quarter(src, dst, sem, c):
+        return [
+            pltpu.make_async_copy(src.at[pl.ds(8 * c + h, 8)], dst.at[pl.ds(8 * c + h, 8)], sem.at[c, h // 32])
+            for h in (0, 32)
+        ]
+
+    for copy in small_copies + [copy for c in range(4) for copy in quarter(pair_hbm, pair, pair_sem, c)]:
+        copy.start()
     row, col, ka = lax.axis_index("row"), lax.axis_index("col"), lax.axis_index("ka")
     core = lax.rem(ka, 2)
     x, z = (ka // 2) * 2 + row // 8, lax.rem(row, 8)
@@ -51,13 +70,23 @@
 
     barrier = pltpu.get_barrier_semaphore()
 
-    def greet(step, _):
-        pl.semaphore_signal(barrier, inc=1, device_id=partner(step)[1], device_id_type=MESH)
-        return 0
-
-    lax.fori_loop(1, CHIPS, greet, 0)
+    def line(axis, d):
+        tz = lax.rem(z + d, 8) if axis == "z" else z
+        tx = lax.rem(x + d, 4) if axis == "x" else x
+        ty = lax.rem(col + d, 4) if axis == "y" else col
+        return (lax.rem(tx, 2) * 8 + tz, ty, (tx // 2) * 2 + core)
+
+    def greet(sem, axis, count):
+        for d in range(1, count):
+            pl.semaphore_signal(sem, inc=1, device_id=line(axis, d), device_id_type=MESH)
+
+    greet(barrier, "z", 8)
+    greet(barrier, "x", 4)
+    greet(barrier, "y", 4)
     pl.semaphore_signal(barrier, inc=1, device_id=sibling, device_id_type=MESH)
 
+    for copy in small_copies:
+        copy.wait()
     rows = [in_gain[...], in_shift[...]]
     rows += [inner_bias[:, 128 * i : 128 * i + 128] for i in range(4)]
     rows += [gate_bias[...], out_gain[...], out_shift[...], out_bias[...]]
@@ -81,8 +110,20 @@
             flat[pl.ds(at + 128, 128), :] = right[:, half * 128 : half * 128 + 128]
         return 0
 
-    lax.fori_loop(0, 16, project, 0)
-    pl.semaphore_wait(barrier, CHIPS)
+    def project_quarter(c):
+        for copy in quarter(pair_hbm, pair, pair_sem, c):
+            copy.wait()
+        lax.fori_loop(4 * c, 4 * c + 4, project, 0, unroll=4)
+
+    project_quarter(0)
+    project_quarter(1)
+    pl.semaphore_wait(barrier, 14)
+    greet(plane_sem, "x", 4)
+    project_quarter(2)
+    pl.semaphore_wait(plane_sem, 3)
+    greet(all_sem, "y", 4)
+    project_quarter(3)
+    pl.semaphore_wait(all_sem, 3)
 
     def channel(h):
         l = flat[pl.ds(h, 32, stride=256), :]
@@ -105,7 +146,7 @@
         gate[r] = sigmoid(g)
         return 0
 
-    lax.fori_loop(0, 16, gates, 0)
+    lax.fori_loop(0, 16, gates, 0, unroll=2)
 
     others = pl.ds(0, CHIPS - 1)
     pltpu.make_async_copy(recv1.at[others], recv1.at[others], recv1_sem).wait()
@@ -205,24 +246,34 @@
         out[r0 + 33] = update[192:]
         return 0
 
-    lax.fori_loop(0, 16, finish, 0)
+    for c in range(4):
+        lax.fori_loop(4 * c, 4 * c + 4, finish, 0, unroll=4)
+        for copy in quarter(out, out_hbm, out_sem, c):
+            copy.start()
 
     pltpu.make_async_copy(send1.at[others], send1.at[others], send1_sem).wait()
     pltpu.make_async_copy(send2.at[others], send2.at[others], send2_sem).wait()
     for g in range(4):
         part_copy(g).wait_send()
+    for c in range(4):
+        for copy in quarter(out, out_hbm, out_sem, c):
+            copy.wait()
 
 
 def on_device(pair, in_gain, in_shift, w_inner, inner_bias, gate_weight, gate_bias, out_gain, out_shift, out_weight, out_bias):
-    vmem = pl.BlockSpec(memory_space=pltpu.VMEM)
+    anywhere = pl.BlockSpec(memory_space=pl.ANY)
     dma = pltpu.SemaphoreType.DMA
     as_row = lambda v: v.reshape(1, -1)
     return pl.pallas_call(
         kernel,
         out_shape=jax.ShapeDtypeStruct((64, 64, 128), BF16),
-        in_specs=[vmem] * 11,
-        out_specs=vmem,
+        in_specs=[anywhere] * 11,
+        out_specs=anywhere,
         scratch_shapes=[
+            *(pltpu.VMEM(shape, dtype) for shape, dtype in SMALL),
+            pltpu.VMEM((64, 64, 128), BF16),
+            pltpu.VMEM((64, 64, 128), BF16),
+            dma((10,)), dma((4, 2)), dma((4, 2)), pltpu.SemaphoreType.REGULAR, pltpu.SemaphoreType.REGULAR,
             pltpu.VMEM((10, 128, 128), F32),
             pltpu.VMEM((512, 128), BF16),
             pltpu.VMEM((128, 128), BF16),
@@ -242,7 +293,7 @@
             dma, dma, dma((4,)), dma((4,)), dma, dma,
         ],
         compiler_params=pltpu.CompilerParams(
-            collective_id=0, has_side_effects=True, vmem_limit_bytes=40 * 2**20
+            collective_id=0, has_side_effects=True, vmem_limit_bytes=56 * 2**20
         ),
     )(
         pair, as_row(in_gain), as_row(in_shift), w_inner, as_row(inner_bias), gate_weight, as_row(gate_bias),

time: 109 us -> 99.6 us (0.914); the launches traced: 109 us -> 98.2 us
  Pallas kernels: 104 us -> 95.9 us
  local copies, waits for them, and re-layouts: 5.33 us -> 2.26 us
    pallas_call x1, Pallas kernels: 104 us -> 95.9 us  [on_device(): pl.pallas_call(kernel, out_shape=jax.ShapeDtypeStruct((64, 64, 128), BF16...]
    unnamed x23 -> x1, local copies, waits for them, and re-layouts: 5.33 us -> 2.26 us
where the time goes in v2:
time: 99.6 us; the launch traced here: 98.2 us
  Pallas kernels  95.9 us (96%)
  local copies, waits for them, and re-layouts  2.26 us (2%)
    pallas_call x1, Pallas kernels, on_device(): pl.pallas_call(kernel, out_shape=jax.ShapeDtypeStruct((64, 64, 128), BF16...  95.9 us
    unnamed x1, local copies, waits for them, and re-layouts  2.26 us

profile of v2, /device:TPU:6, one launch (start us, length us, event | category | flops | bytes accessed | tf_op | source)
XLA Modules:
  0.0 98.2 jit_solution(12669303632464896704)
XLA Ops:
  0.0 95.9 %shard_map.109 = bf16[64,64,128]{2,1,0:T(8,128)(2,1)} custom-call(bf16[64,64,128]{2,1,0:T(8,128)(2,1)} %pair_hbm.1, f32[1,128]{1,0:T(1,128)} %bitcast.8, f32[1,128]{1,0:T(1,128)} %bitcast.9, bf16[128,512]{1,0:T(8,128)(2,1)} %refs_2_.1, f32[1,512]{1,0:T(1,128)} %bitcast.7, bf16[128,128]{1,0:T(8,128)(2,1)} %refs_4_.1, f32[1,128]{1,0:T(1,128)} %bitcast.10, ...), custom_call_target="tpu_custom_call" | custom-call | tf_op jit(solution)/shard_map/pallas_call | solution.py:267
  95.9 2.3 %copy.13 = bf16[64,64,128]{2,1,0:T(8,128)(2,1)} copy(bf16[64,64,128]{2,1,0:T(8,128)(2,1)} %shard_map.109) | data formatting | bytes 2097152

commit v3 on v2

v3 whole, which is shorter than its diff:
```python
import functools

import jax
import jax.numpy as jnp
from jax import lax
from jax.experimental import pallas as pl
from jax.experimental.pallas import tpu as pltpu
from jax.sharding import PartitionSpec as P

MESH = pl.DeviceIdType.MESH
CHIPS = 128
ROWS = 16
BF16, F32 = jnp.bfloat16, jnp.float32
SMALL = [
    ((1, 128), F32), ((1, 128), F32), ((128, 512), BF16), ((1, 512), F32), ((128, 128), BF16),
    ((1, 128), F32), ((1, 128), F32), ((1, 128), F32), ((128, 128), BF16), ((1, 128), F32),
]
NT = (((1,), (1,)), ((), ()))


def sigmoid(x):
    return 0.5 * jnp.tanh(0.5 * x) + 0.5


def normalise(x, gain, shift):
    mean = jnp.sum(x, axis=0, keepdims=True) * (1.0 / 128)
    centred = x - mean
    variance = jnp.sum(centred * centred, axis=0, keepdims=True) * (1.0 / 128)
    return centred * lax.rsqrt(variance + 1e-05) * gain + shift


def twice(column):
    return jnp.concatenate([column, column], axis=1)


def kernel(
    pair_hbm, *refs
):
    small_hbm, out_hbm, refs = refs[:10], refs[10], refs[11:]
    small, refs = refs[:10], refs[10:]
    in_gain, in_shift, w_inner, inner_bias, gate_weight, gate_bias, out_gain, out_shift, out_weight, out_bias = small
    (
    pair, out, small_sem, pair_sem, out_sem, plane_sem, all_sem,
    cols, w_t, gw_t, ow_t, flat, normed, send_l, recv_l, send_r, recv_r, left_m, right_m, acc, part_out, part_in,
    send2, recv2, gate,
    send_l_sem, recv_l_sem, send_r_sem, recv_r_sem, part_send_sem, part_recv_sem, send2_sem, recv2_sem,
    ) = refs
    small_copies = [pltpu.make_async_copy(a, b, small_sem.at[i]) for i, (a, b) in enumerate(zip(small_hbm, small))]

    def quarter(src, dst, sem, c):
        return [
            pltpu.make_async_copy(src.at[pl.ds(8 * c + h, 8)], dst.at[pl.ds(8 * c + h, 8)], sem.at[c, h // 32])
            for h in (0, 32)
        ]

    for copy in small_copies + [copy for c in range(4) for copy in quarter(pair_hbm, pair, pair_sem, c)]:
        copy.start()
    row, col, ka = lax.axis_index("row"), lax.axis_index("col"), lax.axis_index("ka")
    core = lax.rem(ka, 2)
    x_hi, x_lo = lax.div(ka, 2), lax.div(row, 8)
    x, z = x_hi * 2 + x_lo, lax.rem(row, 8)
    me = (col * 2 + x_hi) * ROWS + row

    z_at = [lax.rem(z + d, 8) for d in range(8)]

    def partners(dx, dy, dzs):
        tx, ty = lax.rem(x + dx, 4), lax.rem(col + dy, 4)
        hi = lax.div(tx, 2)
        lo = (tx - 2 * hi) * 8
        base, ka_to = (ty * 2 + hi) * ROWS + lo, hi * 2 + core
        return [(base + z_at[d], (lo + z_at[d], ty, ka_to)) for d in dzs]

    sibling = (row, col, x_hi * 2 + 1 - core)

    barrier = pltpu.get_barrier_semaphore()

    def line(axis, d):
        tz = lax.rem(z + d, 8) if axis == "z" else z
        tx = lax.rem(x + d, 4) if axis == "x" else x
        ty = lax.rem(col + d, 4) if axis == "y" else col
        return (lax.rem(tx, 2) * 8 + tz, ty, (tx // 2) * 2 + core)

    def greet(sem, axis, count):
        for d in range(1, count):
            pl.semaphore_signal(sem, inc=1, device_id=line(axis, d), device_id_type=MESH)

    greet(barrier, "z", 8)
    greet(barrier, "x", 4)
    greet(barrier, "y", 4)
    pl.semaphore_signal(barrier, inc=1, device_id=sibling, device_id_type=MESH)

    for copy in small_copies:
        copy.wait()
    rows = [in_gain[...], in_shift[...]]
    rows += [inner_bias[:, 128 * i : 128 * i + 128] for i in range(4)]
    rows += [gate_bias[...], out_gain[...], out_shift[...], out_bias[...]]
    for i, values in enumerate(rows):
        cols[i] = jnp.broadcast_to(values, (128, 128)).T
    w_t[...] = w_inner[...].astype(F32).T.astype(BF16)
    gw_t[...] = gate_weight[...].astype(F32).T.astype(BF16)
    ow_t[...] = out_weight[...].astype(F32).T.astype(BF16)

    def project(r, _):
        r0 = 2 * r
        block = jnp.concatenate([pair[r0], pair[r0 + 32], pair[r0 + 1], pair[r0 + 33]], axis=0)
        n = normalise(block.astype(F32).T, twice(cols[0]), twice(cols[1])).astype(BF16)
        normed[r] = n
        inner = jnp.dot(w_t[...], n, preferred_element_type=F32)
        left = sigmoid(inner[128:256] + twice(cols[3])) * (inner[:128] + twice(cols[2]))
        right = sigmoid(inner[384:] + twice(cols[5])) * (inner[256:384] + twice(cols[4]))
        for half in range(2):
            at = pl.multiple_of((r0 + half) * 256, 256)
            flat[pl.ds(at, 128), :] = left[:, half * 128 : half * 128 + 128]
            flat[pl.ds(at + 128, 128), :] = right[:, half * 128 : half * 128 + 128]
        return 0

    def project_quarter(c):
        for copy in quarter(pair_hbm, pair, pair_sem, c):
            copy.wait()
        lax.fori_loop(4 * c, 4 * c + 4, project, 0, unroll=4)

    def channel(first, h):
        return flat[pl.ds(first + h, 32, stride=256), :].astype(BF16)

    def send_left(dx, dy, dzs=(0, 4, 1, 7, 2, 6, 3, 5)):
        for chip, device in partners(dx, dy, dzs):
            send_l[chip] = channel(0, chip)
            pltpu.make_async_remote_copy(
                send_l.at[chip], recv_l.at[me], send_l_sem, recv_l_sem, device_id=device, device_id_type=MESH
            ).start()
        return 0

    def z_steps(g):
        return (g, 8 - g) if g else (0, 4)

    def send_right(g):
        def send(dy, first):
            for dx in range(4):
                for chip, device in partners(dx, dy, z_steps(g)[1 if first and dx == 0 else 0 :]):
                    send_r[chip] = channel(128, chip)
                    pltpu.make_async_remote_copy(
                        send_r.at[chip], recv_r.at[me], send_r_sem, recv_r_sem.at[g],
                        device_id=device, device_id_type=MESH,
                    ).start()
            return 0

        if g == 0:
            send(0, True)
        lax.fori_loop(0 if g else 1, 4, lambda dy, _: send(dy, False), 0)

    project_quarter(0)
    project_quarter(1)
    pl.semaphore_wait(barrier, 14)
    greet(plane_sem, "x", 4)
    project_quarter(2)
    project_quarter(3)
    send_left(0, 0, (4, 1, 7, 2, 6, 3, 5))
    pl.semaphore_wait(plane_sem, 3)
    greet(all_sem, "y", 4)
    lax.fori_loop(1, 4, lambda dx, _: send_left(dx, 0), 0)
    pl.semaphore_wait(all_sem, 3)
    lax.fori_loop(1, 4, lambda dy, _: lax.fori_loop(0, 4, lambda dx, _: send_left(dx, dy), 0), 0)
    for g in range(4):
        send_right(g)
    recv_l[me] = channel(0, me)
    recv_r[me] = channel(128, me)

    def gates(r, _):
        g = jnp.dot(gw_t[...], normed[r], preferred_element_type=F32) + twice(cols[6])
        gate[r] = sigmoid(g)
        return 0

    lax.fori_loop(0, 16, gates, 0, unroll=2)

    others = pl.ds(0, CHIPS - 1)
    pltpu.make_async_copy(recv_l.at[others], recv_l.at[others], recv_l_sem).wait()

    def assemble(src, b, dst, at):
        for p in range(4):
            one, two = src[2 * p * ROWS + b], src[(2 * p + 1) * ROWS + b]
            k = slice(p * 128, p * 128 + 128)
            dst[pl.ds(at, 32), k] = jnp.concatenate([one[:, :64], two[:, :64]], axis=1)
            dst[pl.ds(at + 32, 32), k] = jnp.concatenate([one[:, 64:], two[:, 64:]], axis=1)

    def assemble_left(b, _):
        assemble(recv_l, b, left_m, pl.multiple_of(b * 64, 64))
        return 0

    lax.fori_loop(0, ROWS, assemble_left, 0)

    def part_copy(slot, m):
        return pltpu.make_async_remote_copy(
            part_out.at[slot, m], part_in.at[slot, m], part_send_sem.at[slot, m], part_recv_sem.at[slot, m],
            device_id=sibling, device_id_type=MESH,
        )

    def multiply(g):
        one, two = z_steps(g)
        slot = g // 2
        some = pl.ds(0, 32 if g else 31)
        pltpu.make_async_copy(recv_r.at[some], recv_r.at[some], recv_r_sem.at[g]).wait()
        zs = [z_at[one], z_at[two]]
        kbs = [(n // 2) * 4 + lax.div(zs[n % 2], 2) for n in range(4)]
        homes = [(lax.div(kb, 2), lax.rem(kb, 2) * 2 + core) for kb in kbs]
        for n in range(4):
            assemble(recv_r, (n // 2) * 8 + zs[n % 2], right_m, n * 64)

        def product(m):
            lhs = left_m[pl.ds(pl.multiple_of(m * 256, 256), 256), :]
            return lax.dot_general(lhs, right_m[...], NT, preferred_element_type=F32)

        own = lax.rem(z + g, 2) == core

        @pl.when(jnp.logical_not(own))
        def _():
            def for_sibling(m, _):
                part_out[slot, m] = product(m).astype(BF16)
                part_copy(slot, m).start()
                return 0

            lax.fori_loop(0, 4, for_sibling, 0)

        @pl.when(own)
        def _():
            def for_us(m, _):
                acc[m] = product(m)
                return 0

            lax.fori_loop(0, 4, for_us, 0)

            def tiles(m, _):
                part_copy(slot, m).wait_recv()
                tri = (acc[m] + part_in[slot, m].astype(F32)).astype(BF16)
                for b in range(4):
                    for n in range(4):
                        low = tri[b * 64 : b * 64 + 32, n * 64 : n * 64 + 64]
                        high = tri[b * 64 + 32 : b * 64 + 64, n * 64 : n * 64 + 64]
                        send2[kbs[n] * ROWS + m * 4 + b] = jnp.concatenate([low, high], axis=1)
                return 0

            lax.fori_loop(0, 4, tiles, 0)

            def give_back(a, half, here):
                part = slice(half * 16, half * 16 + 16)
                tz = lax.rem(z + 3 * a, 8)
                for n in range(4):
                    for lo in (0, 8):
                        chip, device = kbs[n] * ROWS + lo + tz, (lo + tz, *homes[n])
                        copy = pltpu.make_async_remote_copy(
                            send2.at[chip, part], recv2.at[me, part], send2_sem, recv2_sem.at[half],
                            device_id=device, device_id_type=MESH,
                        )
                        if not here:
                            copy.start()
                            continue

                        @pl.when(chip == me)
                        def _():
                            recv2[me, part] = send2[me, part]

                        @pl.when(chip != me)
                        def _():
                            copy.start()

                return 0

            for half in range(2):
                lax.fori_loop(1, 8, lambda a, _: give_back(a, half, False), 0)
                give_back(0, half, True)

    for g in range(4):
        multiply(g)

    def widen(half):
        def one(h, _):
            at = pl.multiple_of(h * 32 + half * 16, 16)
            flat[pl.ds(at, 16), :] = recv2[h, pl.ds(half * 16, 16)].astype(F32)
            return 0

        return one

    def finish(r, _):
        r0 = 2 * r
        t = jnp.concatenate(
            [flat[pl.ds(r0, 128, stride=32), :], flat[pl.ds(r0 + 1, 128, stride=32), :]], axis=1
        )
        n = normalise(t, twice(cols[7]), twice(cols[8])).astype(BF16)
        projected = jnp.dot(ow_t[...], n, preferred_element_type=F32) + twice(cols[9])
        update = (gate[r] * projected).T.astype(BF16)
        out[r0] = update[:64]
        out[r0 + 32] = update[64:128]
        out[r0 + 1] = update[128:192]
        out[r0 + 33] = update[192:]
        return 0

    for half in range(2):
        rows_in = recv2.at[others, pl.ds(half * 16, 16)]
        pltpu.make_async_copy(rows_in, rows_in, recv2_sem.at[half]).wait()
        lax.fori_loop(0, CHIPS, widen(half), 0, unroll=4)
        for c in (2 * half, 2 * half + 1):
            lax.fori_loop(4 * c, 4 * c + 4, finish, 0, unroll=4)
            for copy in quarter(out, out_hbm, out_sem, c):
                copy.start()

    pltpu.make_async_copy(send_l.at[others], send_l.at[others], send_l_sem).wait()
    pltpu.make_async_copy(send_r.at[others], send_r.at[others], send_r_sem).wait()
    pltpu.make_async_copy(send2.at[others], send2.at[others], send2_sem).wait()
    for g in range(4):

        @pl.when(lax.rem(z + g, 2) != core)
        def _():
            for m in range(4):
                part_copy(g // 2, m).wait_send()

    for c in range(4):
        for copy in quarter(out, out_hbm, out_sem, c):
            copy.wait()


def on_device(pair, in_gain, in_shift, w_inner, inner_bias, gate_weight, gate_bias, out_gain, out_shift, out_weight, out_bias):
    anywhere = pl.BlockSpec(memory_space=pl.ANY)
    dma = pltpu.SemaphoreType.DMA
    as_row = lambda v: v.reshape(1, -1)
    return pl.pallas_call(
        kernel,
        out_shape=jax.ShapeDtypeStruct((64, 64, 128), BF16),
        in_specs=[anywhere] * 11,
        out_specs=anywhere,
        scratch_shapes=[
            *(pltpu.VMEM(shape, dtype) for shape, dtype in SMALL),
            pltpu.VMEM((64, 64, 128), BF16),
            pltpu.VMEM((64, 64, 128), BF16),
            dma((10,)), dma((4, 2)), dma((4, 2)), pltpu.SemaphoreType.REGULAR, pltpu.SemaphoreType.REGULAR,
            pltpu.VMEM((10, 128, 128), F32),
            pltpu.VMEM((512, 128), BF16),
            pltpu.VMEM((128, 128), BF16),
            pltpu.VMEM((128, 128), BF16),
            pltpu.VMEM((32 * 256, 128), F32),
            pltpu.VMEM((16, 128, 256), BF16),
            *[pltpu.VMEM((CHIPS, 32, 128), BF16)] * 4,
            pltpu.VMEM((1024, 512), BF16),
            pltpu.VMEM((256, 512), BF16),
            pltpu.VMEM((4, 256, 256), F32),
            *[pltpu.VMEM((2, 4, 256, 256), BF16)] * 2,
            *[pltpu.VMEM((CHIPS, 32, 128), BF16)] * 2,
            pltpu.VMEM((16, 128, 256), F32),
            dma, dma, dma, dma((4,)), dma((2, 4)), dma((2, 4)), dma, dma((2,)),
        ],
        compiler_params=pltpu.CompilerParams(
            collective_id=0, has_side_effects=True, vmem_limit_bytes=56 * 2**20
        ),
    )(
        pair, as_row(in_gain), as_row(in_shift), w_inner, as_row(inner_bias), gate_weight, as_row(gate_bias),
        as_row(out_gain), as_row(out_shift), out_weight, as_row(out_bias),
    )


def solution(mesh):
    placed = (P("row", ("col", "ka"), None),) + (P(),) * 10
    return jax.shard_map(
        on_device, mesh=mesh, in_specs=placed, out_specs=P("row", ("col", "ka"), None), check_vma=False
    )
```

time: 99.6 us -> 87.9 us (0.88)
  Pallas kernels: 95.9 us -> 84.6 us
    pallas_call x1, Pallas kernels: 95.9 us -> 84.6 us  [on_device(): pl.pallas_call(kernel, out_shape=jax.ShapeDtypeStruct((64, 64, 128), BF16...]
where the time goes in v3:
time: 87.9 us; the launch traced here: 86.8 us
  Pallas kernels  84.6 us (96%)
  local copies, waits for them, and re-layouts  2.26 us (3%)
    pallas_call x1, Pallas kernels, on_device(): pl.pallas_call(kernel, out_shape=jax.ShapeDtypeStruct((64, 64, 128), BF16...  84.6 us
    unnamed x1, local copies, waits for them, and re-layouts  2.26 us

profile of v3, /device:TPU:6, one launch (start us, length us, event | category | flops | bytes accessed | tf_op | source)
XLA Modules:
  0.0 86.8 jit_solution(10786788936025999393)
XLA Ops:
  0.0 84.6 %shard_map.109 = bf16[64,64,128]{2,1,0:T(8,128)(2,1)} custom-call(bf16[64,64,128]{2,1,0:T(8,128)(2,1)} %pair_hbm.1, f32[1,128]{1,0:T(1,128)} %bitcast.8, f32[1,128]{1,0:T(1,128)} %bitcast.9, bf16[128,512]{1,0:T(8,128)(2,1)} %refs_2_.1, f32[1,512]{1,0:T(1,128)} %bitcast.7, bf16[128,128]{1,0:T(8,128)(2,1)} %refs_4_.1, f32[1,128]{1,0:T(1,128)} %bitcast.10, ...), custom_call_target="tpu_custom_call" | custom-call | tf_op jit(solution)/shard_map/pallas_call | solution.py:324
  84.6 2.3 %copy.13 = bf16[64,64,128]{2,1,0:T(8,128)(2,1)} copy(bf16[64,64,128]{2,1,0:T(8,128)(2,1)} %shard_map.109) | data formatting | bytes 2097152

commit v4 on v3

v4 whole, which is shorter than its diff:
```python
import functools

import jax
import jax.numpy as jnp
from jax import lax
from jax.experimental import pallas as pl
from jax.experimental.pallas import tpu as pltpu
from jax.sharding import PartitionSpec as P

MESH = pl.DeviceIdType.MESH
CHIPS = 128
ROWS = 16
BF16, F32 = jnp.bfloat16, jnp.float32
SMALL = [
    ((1, 128), F32), ((1, 128), F32), ((128, 512), BF16), ((1, 512), F32), ((128, 128), BF16),
    ((1, 128), F32), ((1, 128), F32), ((1, 128), F32), ((128, 128), BF16), ((1, 128), F32),
]
NT = (((1,), (1,)), ((), ()))


def sigmoid(x):
    return 0.5 * jnp.tanh(0.5 * x) + 0.5


def normalise(x, gain, shift):
    mean = jnp.sum(x, axis=0, keepdims=True) * (1.0 / 128)
    centred = x - mean
    variance = jnp.sum(centred * centred, axis=0, keepdims=True) * (1.0 / 128)
    return centred * lax.rsqrt(variance + 1e-05) * gain + shift


def twice(column):
    return jnp.concatenate([column, column], axis=1)


def kernel(
    pair_hbm, *refs
):
    small_hbm, out_hbm, refs = refs[:10], refs[10], refs[11:]
    small, refs = refs[:10], refs[10:]
    in_gain, in_shift, w_inner, inner_bias, gate_weight, gate_bias, out_gain, out_shift, out_weight, out_bias = small
    (
    pair, out, small_sem, pair_sem, out_sem, plane_sem, all_sem,
    cols, w_t, gw_t, ow_t, flat, normed, send_l, recv_l, send_r, recv_r, passed, left_m, right_m, acc, part_out, part_in,
    send2, recv2, gate,
    send_l_sem, recv_l_sem, send_r_sem, recv_r_sem, pass_send_sem, pass_recv_sem, part_send_sem, part_recv_sem, send2_sem, recv2_sem,
    ) = refs
    small_copies = [pltpu.make_async_copy(a, b, small_sem.at[i]) for i, (a, b) in enumerate(zip(small_hbm, small))]

    def quarter(src, dst, sem, c):
        return [
            pltpu.make_async_copy(src.at[pl.ds(8 * c + h, 8)], dst.at[pl.ds(8 * c + h, 8)], sem.at[c, h // 32])
            for h in (0, 32)
        ]

    row, col, ka = lax.axis_index("row"), lax.axis_index("col"), lax.axis_index("ka")
    core = lax.rem(ka, 2)
    x_hi, x_lo = lax.div(ka, 2), lax.div(row, 8)
    x, z = x_hi * 2 + x_lo, lax.rem(row, 8)
    me = (col * 2 + x_hi) * ROWS + row

    z_at = [lax.rem(z + d, 8) for d in range(8)]

    mine = (me, me - z + z_at[7])
    place = x_lo * 8 + col * 2 + x_hi

    def partners(dx, dy, ds):
        tx, ty = lax.rem(x + dx, 4), lax.rem(col + dy, 4)
        hi = lax.div(tx, 2)
        lo = (tx - 2 * hi) * 8
        base, ka_to = (ty * 2 + hi) * ROWS + lo, hi * 2 + core
        return [
            (base + z_at[d], (lo + z_at[d if d < 4 else (d + 1) % 8], ty, ka_to), (d if d < 4 else 11 - d) * 16 + place)
            for d in ds
        ]

    sibling = (row, col, x_hi * 2 + 1 - core)

    barrier = pltpu.get_barrier_semaphore()

    def line(axis, d):
        tz = lax.rem(z + d, 8) if axis == "z" else z
        tx = lax.rem(x + d, 4) if axis == "x" else x
        ty = lax.rem(col + d, 4) if axis == "y" else col
        return (lax.rem(tx, 2) * 8 + tz, ty, (tx // 2) * 2 + core)

    def greet(sem, axis, count):
        for d in range(1, count):
            pl.semaphore_signal(sem, inc=1, device_id=line(axis, d), device_id_type=MESH)

    greet(barrier, "z", 8)
    greet(barrier, "x", 4)
    greet(barrier, "y", 4)
    pl.semaphore_signal(barrier, inc=1, device_id=sibling, device_id_type=MESH)

    for copy in small_copies + [copy for c in range(4) for copy in quarter(pair_hbm, pair, pair_sem, c)]:
        copy.start()
    rows = [(in_gain, 0), (in_shift, 0), *((inner_bias, 128 * i) for i in range(4))]
    rows += [(gate_bias, 0), (out_gain, 0), (out_shift, 0), (out_bias, 0)]

    def columns(which):
        for i in which:
            ref, at = rows[i]
            cols[i] = jnp.broadcast_to(ref[:, at : at + 128], (128, 128)).T

    def turned(weight):
        return weight.astype(F32).T.astype(BF16)

    def branch(n, first):
        inner = jnp.dot(w_t[first * 128 : first * 128 + 256], n, preferred_element_type=F32)
        return sigmoid(inner[128:] + twice(cols[first + 3])) * (inner[:128] + twice(cols[first + 2]))

    def keep(values, r, first):
        for half in range(2):
            at = pl.multiple_of((2 * r + half) * 256 + first, 128)
            flat[pl.ds(at, 128), :] = values[:, half * 128 : half * 128 + 128]

    def project_left(r, _):
        r0 = 2 * r
        block = jnp.concatenate([pair[r0], pair[r0 + 32], pair[r0 + 1], pair[r0 + 33]], axis=0)
        n = normalise(block.astype(F32).T, twice(cols[0]), twice(cols[1])).astype(BF16)
        normed[r] = n
        keep(branch(n, 0), r, 0)
        return 0

    def project_right(r, _):
        keep(branch(normed[r], 2), r, 128)
        return 0

    def left_quarter(c):
        for copy in quarter(pair_hbm, pair, pair_sem, c):
            copy.wait()
        lax.fori_loop(4 * c, 4 * c + 4, project_left, 0, unroll=4)

    def channel(first, h):
        return flat[pl.ds(first + h, 32, stride=256), :].astype(BF16)

    def send_left(dx, dy, ds=(0, 7, 1, 6, 2, 5, 3, 4)):
        for chip, device, slot in partners(dx, dy, ds):
            send_l[chip] = channel(0, chip)
            pltpu.make_async_remote_copy(
                send_l.at[chip], recv_l.at[slot], send_l_sem, recv_l_sem, device_id=device, device_id_type=MESH
            ).start()
        return 0

    def send_right(j):
        def send(dy, dxs):
            for dx in dxs:
                for chip, device, slot in partners(dx, dy, (j, 7 - j)):
                    send_r[chip] = channel(128, chip)
                    pltpu.make_async_remote_copy(
                        send_r.at[chip], recv_r.at[slot], send_r_sem, recv_r_sem.at[j],
                        device_id=device, device_id_type=MESH,
                    ).start()
            return 0

        if j == 0:
            send(0, (1, 2, 3))
        lax.fori_loop(0 if j else 1, 4, lambda dy, _: send(dy, range(4)), 0)

    for i in (0, 1, 2, 3):
        small_copies[i].wait()
    columns(range(4))
    w_t[:256] = turned(w_inner[:, :256])
    left_quarter(0)
    left_quarter(1)
    pl.semaphore_wait(barrier, 14)
    greet(plane_sem, "x", 4)
    left_quarter(2)
    left_quarter(3)
    send_left(0, 0, (1, 6, 2, 5, 3, 4))
    pl.semaphore_wait(plane_sem, 3)
    greet(all_sem, "y", 4)
    lax.fori_loop(1, 4, lambda dx, _: send_left(dx, 0), 0)
    for copy in small_copies[4:]:
        copy.wait()
    columns(range(4, 10))
    w_t[256:] = turned(w_inner[:, 256:])
    gw_t[...] = turned(gate_weight[...])
    ow_t[...] = turned(out_weight[...])
    lax.fori_loop(0, 16, project_right, 0, unroll=4)
    pl.semaphore_wait(all_sem, 3)
    lax.fori_loop(1, 4, lambda dy, _: lax.fori_loop(0, 4, lambda dx, _: send_left(dx, dy), 0), 0)
    for role in range(2):
        recv_l[role * 64 + place] = channel(0, mine[role])
        recv_r[role * 64 + place] = channel(128, mine[role])
    for j in range(4):
        send_right(j)

    def gates(r, _):
        g = jnp.dot(gw_t[...], normed[r], preferred_element_type=F32) + twice(cols[6])
        gate[r] = sigmoid(g)
        return 0

    lax.fori_loop(0, 16, gates, 0, unroll=2)

    others = pl.ds(0, CHIPS - 2)
    pltpu.make_async_copy(recv_l.at[others], recv_l.at[others], recv_l_sem).wait()

    def assemble(src, b, dst, at):
        for p in range(4):
            one, two = src[b * 8 + 2 * p], src[b * 8 + 2 * p + 1]
            k = slice(p * 128, p * 128 + 128)
            dst[pl.ds(at, 32), k] = jnp.concatenate([one[:, :64], two[:, :64]], axis=1)
            dst[pl.ds(at + 32, 32), k] = jnp.concatenate([one[:, 64:], two[:, 64:]], axis=1)

    def assemble_left(b, _):
        assemble(recv_l, b, left_m, pl.multiple_of(b * 64, 64))
        return 0

    lax.fori_loop(0, ROWS, assemble_left, 0)

    def pass_copy(role, j):
        return pltpu.make_async_remote_copy(
            recv_r.at[pl.ds((role * 4 + j) * 16, 16)], passed.at[pl.ds(((1 - role) * 4 + j) * 16, 16)],
            pass_send_sem.at[role, j], pass_recv_sem.at[1 - role, j],
            device_id=line("z", 7 if role else 1), device_id_type=MESH,
        )

    def passed_here(role, j):
        ref = passed.at[pl.ds((role * 4 + j) * 16, 16)]
        return pltpu.make_async_copy(ref, ref, pass_recv_sem.at[role, j])

    def part_copy(t, m):
        columns = pl.ds(0, 256 if 0 < t < 4 else 128)
        return pltpu.make_async_remote_copy(
            part_out.at[t // 2, m, :, columns], part_in.at[t // 2, m, :, columns],
            part_send_sem.at[t // 2, m], part_recv_sem.at[t // 2, m], device_id=sibling, device_id_type=MESH,
        )

    def multiply(t):
        if t < 4:
            some = pl.ds(0, 32 if t else 30)
            pltpu.make_async_copy(recv_r.at[some], recv_r.at[some], recv_r_sem.at[t]).wait()
            for role in range(2):
                pass_copy(role, t).start()
        if t > 0:
            for role in range(2):
                passed_here(role, t - 1).wait()
        planes = [z_at[8 - t], z_at[t]] if 0 < t < 4 else [z_at[t]]
        blocks = 2 * len(planes)
        width = 64 * blocks
        kbs = [(n % 2) * 4 + lax.div(planes[n // 2], 2) for n in range(blocks)]
        homes = [(lax.div(kb, 2), lax.rem(kb, 2) * 2 + core) for kb in kbs]
        for role in range(2):
            for n in range(blocks):
                direct = t == 0 or (t < 4 and n // 2 == role)
                src, j = (recv_r, t) if direct else (passed, t - 1)
                assemble(src, (role * 4 + j) * 2 + n % 2, right_m, role * 256 + n * 64)

        def product(m):
            lhs = left_m[pl.ds(pl.multiple_of(m * 256, 256), 256), :]
            rhs = right_m[pl.ds(pl.multiple_of(lax.div(m, 2) * 256, 256), width), :]
            return lax.dot_general(lhs, rhs, NT, preferred_element_type=F32)

        own = lax.rem(z + t, 2) == core

        @pl.when(jnp.logical_not(own))
        def _():
            def for_sibling(m, _):
                part_out[t // 2, m, :, :width] = product(m).astype(BF16)
                part_copy(t, m).start()
                return 0

            lax.fori_loop(0, 4, for_sibling, 0)

        @pl.when(own)
        def _():
            def for_us(m, _):
                acc[m, :, :width] = product(m)
                return 0

            lax.fori_loop(0, 4, for_us, 0)

            def tiles(m, _):
                part_copy(t, m).wait_recv()
                tri = (acc[m, :, :width] + part_in[t // 2, m, :, :width].astype(F32)).astype(BF16)
                for b in range(4):
                    for n in range(blocks):
                        low = tri[b * 64 : b * 64 + 32, n * 64 : n * 64 + 64]
                        high = tri[b * 64 + 32 : b * 64 + 64, n * 64 : n * 64 + 64]
                        send2[(m * 4 + b) * 8 + kbs[n]] = jnp.concatenate([low, high], axis=1)
                return 0

            lax.fori_loop(0, 4, tiles, 0)

            def give_back(j, half, here):
                part = slice(half * 16, half * 16 + 16)
                for n in range(blocks):
                    for role, tz in ((0, lax.rem(z + 8 - j, 8)), (1, lax.rem(z + j, 8))):
                        for lo in range(2):
                            tile = ((role * 4 + j) * 2 + lo) * 8 + kbs[n]
                            copy = pltpu.make_async_remote_copy(
                                send2.at[tile, part], recv2.at[mine[role], part], send2_sem, recv2_sem.at[half],
                                device_id=(lo * 8 + tz, *homes[n]), device_id_type=MESH,
                            )
                            if not here:
                                copy.start()
                                continue
                            ours = (kbs[n] * ROWS + lo * 8 + z) == me

                            @pl.when(ours)
                            def _():
                                recv2[mine[role], part] = send2[tile, part]

                            @pl.when(jnp.logical_not(ours))
                            def _():
                                copy.start()

                return 0

            for half in range(2):
                lax.fori_loop(1, 4, lambda j, _: give_back(j, half, False), 0)
                give_back(0, half, True)

    for t in range(5):
        multiply(t)

    def widen(half):
        def one(h, _):
            at = pl.multiple_of(h * 32 + half * 16, 16)
            flat[pl.ds(at, 16), :] = recv2[h, pl.ds(half * 16, 16)].astype(F32)
            return 0

        return one

    def finish(r, _):
        r0 = 2 * r
        t = jnp.concatenate(
            [flat[pl.ds(r0, 128, stride=32), :], flat[pl.ds(r0 + 1, 128, stride=32), :]], axis=1
        )
        n = normalise(t, twice(cols[7]), twice(cols[8])).astype(BF16)
        projected = jnp.dot(ow_t[...], n, preferred_element_type=F32) + twice(cols[9])
        update = (gate[r] * projected).T.astype(BF16)
        out[r0] = update[:64]
        out[r0 + 32] = update[64:128]
        out[r0 + 1] = update[128:192]
        out[r0 + 33] = update[192:]
        return 0

    for half in range(2):
        rows_in = recv2.at[others, pl.ds(half * 16, 16)]
        pltpu.make_async_copy(rows_in, rows_in, recv2_sem.at[half]).wait()
        lax.fori_loop(0, CHIPS, widen(half), 0, unroll=4)
        for c in (2 * half, 2 * half + 1):
            lax.fori_loop(4 * c, 4 * c + 4, finish, 0, unroll=4)
            for copy in quarter(out, out_hbm, out_sem, c):
                copy.start()

    pltpu.make_async_copy(send_l.at[others], send_l.at[others], send_l_sem).wait()
    pltpu.make_async_copy(send_r.at[others], send_r.at[others], send_r_sem).wait()
    pltpu.make_async_copy(send2.at[others], send2.at[others], send2_sem).wait()
    for role in range(2):
        for j in range(4):
            pass_copy(role, j).wait_send()
    for t in range(5):

        @pl.when(lax.rem(z + t, 2) != core)
        def _():
            for m in range(4):
                part_copy(t, m).wait_send()

    for c in range(4):
        for copy in quarter(out, out_hbm, out_sem, c):
            copy.wait()


def on_device(pair, in_gain, in_shift, w_inner, inner_bias, gate_weight, gate_bias, out_gain, out_shift, out_weight, out_bias):
    anywhere = pl.BlockSpec(memory_space=pl.ANY)
    dma = pltpu.SemaphoreType.DMA
    as_row = lambda v: v.reshape(1, -1)
    return pl.pallas_call(
        kernel,
        out_shape=jax.ShapeDtypeStruct((64, 64, 128), BF16),
        in_specs=[anywhere] * 11,
        out_specs=anywhere,
        scratch_shapes=[
            *(pltpu.VMEM(shape, dtype) for shape, dtype in SMALL),
            pltpu.VMEM((64, 64, 128), BF16),
            pltpu.VMEM((64, 64, 128), BF16),
            dma((10,)), dma((4, 2)), dma((4, 2)), pltpu.SemaphoreType.REGULAR, pltpu.SemaphoreType.REGULAR,
            pltpu.VMEM((10, 128, 128), F32),
            pltpu.VMEM((512, 128), BF16),
            pltpu.VMEM((128, 128), BF16),
            pltpu.VMEM((128, 128), BF16),
            pltpu.VMEM((32 * 256, 128), F32),
            pltpu.VMEM((16, 128, 256), BF16),
            *[pltpu.VMEM((CHIPS, 32, 128), BF16)] * 5,
            pltpu.VMEM((1024, 512), BF16),
            pltpu.VMEM((512, 512), BF16),
            pltpu.VMEM((4, 256, 256), F32),
            *[pltpu.VMEM((3, 4, 256, 256), BF16)] * 2,
            *[pltpu.VMEM((CHIPS, 32, 128), BF16)] * 2,
            pltpu.VMEM((16, 128, 256), F32),
            dma, dma, dma, dma((4,)), dma((2, 4)), dma((2, 4)), dma((3, 4)), dma((3, 4)), dma, dma((2,)),
        ],
        compiler_params=pltpu.CompilerParams(
            collective_id=0, has_side_effects=True, vmem_limit_bytes=56 * 2**20
        ),
    )(
        pair, as_row(in_gain), as_row(in_shift), w_inner, as_row(inner_bias), gate_weight, as_row(gate_bias),
        as_row(out_gain), as_row(out_shift), out_weight, as_row(out_bias),
    )


def solution(mesh):
    placed = (P("row", ("col", "ka"), None),) + (P(),) * 10
    return jax.shard_map(
        on_device, mesh=mesh, in_specs=placed, out_specs=P("row", ("col", "ka"), None), check_vma=False
    )
```

time: 87.9 us -> 84.7 us (0.964)
  the two profiles are of different devices: /device:TPU:6 before, /device:TPU:1 now
where the time goes in v4:
time: 84.7 us; the launch traced here: 84.5 us
  Pallas kernels  82.3 us (97%)
  local copies, waits for them, and re-layouts  2.26 us (3%)
    pallas_call x1, Pallas kernels, on_device(): pl.pallas_call(kernel, out_shape=jax.ShapeDtypeStruct((64, 64, 128), BF16...  82.3 us
    unnamed x1, local copies, waits for them, and re-layouts  2.26 us

profile of v4, /device:TPU:1, one launch (start us, length us, event | category | flops | bytes accessed | tf_op | source)
XLA Modules:
  0.0 84.5 jit_solution(11462749409983853022)
XLA Ops:
  0.0 82.3 %shard_map.109 = bf16[64,64,128]{2,1,0:T(8,128)(2,1)} custom-call(bf16[64,64,128]{2,1,0:T(8,128)(2,1)} %pair_hbm.1, f32[1,128]{1,0:T(1,128)} %bitcast.8, f32[1,128]{1,0:T(1,128)} %bitcast.9, bf16[128,512]{1,0:T(8,128)(2,1)} %refs_2_.1, f32[1,512]{1,0:T(1,128)} %bitcast.7, bf16[128,128]{1,0:T(8,128)(2,1)} %refs_4_.1, f32[1,128]{1,0:T(1,128)} %bitcast.10, ...), custom_call_target="tpu_custom_call" | custom-call | tf_op jit(solution)/shard_map/pallas_call | solution.py:372
  82.3 2.3 %copy.13 = bf16[64,64,128]{2,1,0:T(8,128)(2,1)} copy(bf16[64,64,128]{2,1,0:T(8,128)(2,1)} %shard_map.109) | data formatting | bytes 2097152

commit v5 on v4

--- a/solution.py
+++ b/solution.py
@@ -115,41 +115,41 @@
             at = pl.multiple_of((2 * r + half) * 256 + first, 128)
             flat[pl.ds(at, 128), :] = values[:, half * 128 : half * 128 + 128]
 
-    def project_left(r, _):
+    def project_right(r, _):
         r0 = 2 * r
         block = jnp.concatenate([pair[r0], pair[r0 + 32], pair[r0 + 1], pair[r0 + 33]], axis=0)
         n = normalise(block.astype(F32).T, twice(cols[0]), twice(cols[1])).astype(BF16)
         normed[r] = n
-        keep(branch(n, 0), r, 0)
-        return 0
-
-    def project_right(r, _):
-        keep(branch(normed[r], 2), r, 128)
-        return 0
-
-    def left_quarter(c):
+        keep(branch(n, 2), r, 128)
+        return 0
+
+    def project_left(r, _):
+        keep(branch(normed[r], 0), r, 0)
+        return 0
+
+    def right_quarter(c):
         for copy in quarter(pair_hbm, pair, pair_sem, c):
             copy.wait()
-        lax.fori_loop(4 * c, 4 * c + 4, project_left, 0, unroll=4)
+        lax.fori_loop(4 * c, 4 * c + 4, project_right, 0, unroll=4)
 
     def channel(first, h):
         return flat[pl.ds(first + h, 32, stride=256), :].astype(BF16)
 
-    def send_left(dx, dy, ds=(0, 7, 1, 6, 2, 5, 3, 4)):
+    def send_right(dx, dy, ds=(0, 7, 1, 6, 2, 5, 3, 4)):
         for chip, device, slot in partners(dx, dy, ds):
-            send_l[chip] = channel(0, chip)
+            send_r[chip] = channel(128, chip)
             pltpu.make_async_remote_copy(
-                send_l.at[chip], recv_l.at[slot], send_l_sem, recv_l_sem, device_id=device, device_id_type=MESH
+                send_r.at[chip], recv_r.at[slot], send_r_sem, recv_r_sem, device_id=device, device_id_type=MESH
             ).start()
         return 0
 
-    def send_right(j):
+    def send_left(j):
         def send(dy, dxs):
             for dx in dxs:
                 for chip, device, slot in partners(dx, dy, (j, 7 - j)):
-                    send_r[chip] = channel(128, chip)
+                    send_l[chip] = channel(0, chip)
                     pltpu.make_async_remote_copy(
-                        send_r.at[chip], recv_r.at[slot], send_r_sem, recv_r_sem.at[j],
+                        send_l.at[chip], recv_l.at[slot], send_l_sem, recv_l_sem.at[j],
                         device_id=device, device_id_type=MESH,
                     ).start()
             return 0
@@ -160,32 +160,45 @@
 
     for i in (0, 1, 2, 3):
         small_copies[i].wait()
-    columns(range(4))
-    w_t[:256] = turned(w_inner[:, :256])
-    left_quarter(0)
-    left_quarter(1)
+    columns((0, 1, 4, 5))
+    w_t[256:] = turned(w_inner[:, 256:])
+    right_quarter(0)
+    right_quarter(1)
     pl.semaphore_wait(barrier, 14)
     greet(plane_sem, "x", 4)
-    left_quarter(2)
-    left_quarter(3)
-    send_left(0, 0, (1, 6, 2, 5, 3, 4))
+    right_quarter(2)
+    right_quarter(3)
+    send_right(0, 0, (1, 6, 2, 5, 3, 4))
     pl.semaphore_wait(plane_sem, 3)
     greet(all_sem, "y", 4)
-    lax.fori_loop(1, 4, lambda dx, _: send_left(dx, 0), 0)
+    lax.fori_loop(1, 4, lambda dx, _: send_right(dx, 0), 0)
     for copy in small_copies[4:]:
         copy.wait()
-    columns(range(4, 10))
-    w_t[256:] = turned(w_inner[:, 256:])
+    columns((2, 3, 6, 7, 8, 9))
+    w_t[:256] = turned(w_inner[:, :256])
     gw_t[...] = turned(gate_weight[...])
     ow_t[...] = turned(out_weight[...])
-    lax.fori_loop(0, 16, project_right, 0, unroll=4)
+    lax.fori_loop(0, 16, project_left, 0, unroll=4)
     pl.semaphore_wait(all_sem, 3)
-    lax.fori_loop(1, 4, lambda dy, _: lax.fori_loop(0, 4, lambda dx, _: send_left(dx, dy), 0), 0)
+    lax.fori_loop(1, 4, lambda dy, _: lax.fori_loop(0, 4, lambda dx, _: send_right(dx, dy), 0), 0)
     for role in range(2):
         recv_l[role * 64 + place] = channel(0, mine[role])
         recv_r[role * 64 + place] = channel(128, mine[role])
-    for j in range(4):
-        send_right(j)
+    send_left(3)
+
+    def pass_copy(role):
+        return pltpu.make_async_remote_copy(
+            recv_r.at[pl.ds(role * 64, 64)], passed.at[pl.ds((1 - role) * 64, 64)],
+            pass_send_sem.at[role], pass_recv_sem.at[1 - role],
+            device_id=line("z", 7 if role else 1), device_id_type=MESH,
+        )
+
+    others = pl.ds(0, CHIPS - 2)
+    pltpu.make_async_copy(recv_r.at[others], recv_r.at[others], recv_r_sem).wait()
+    for role in range(2):
+        pass_copy(role).start()
+    for j in (2, 1, 0):
+        send_left(j)
 
     def gates(r, _):
         g = jnp.dot(gw_t[...], normed[r], preferred_element_type=F32) + twice(cols[6])
@@ -193,9 +206,6 @@
         return 0
 
     lax.fori_loop(0, 16, gates, 0, unroll=2)
-
-    others = pl.ds(0, CHIPS - 2)
-    pltpu.make_async_copy(recv_l.at[others], recv_l.at[others], recv_l_sem).wait()
 
     def assemble(src, b, dst, at):
         for p in range(4):
@@ -204,116 +214,89 @@
             dst[pl.ds(at, 32), k] = jnp.concatenate([one[:, :64], two[:, :64]], axis=1)
             dst[pl.ds(at + 32, 32), k] = jnp.concatenate([one[:, 64:], two[:, 64:]], axis=1)
 
-    def assemble_left(b, _):
-        assemble(recv_l, b, left_m, pl.multiple_of(b * 64, 64))
-        return 0
-
-    lax.fori_loop(0, ROWS, assemble_left, 0)
-
-    def pass_copy(role, j):
+    def assemble_right(src, role, j, plane):
+        for lo in range(2):
+            at = role * 1024 + lax.rem(plane, 2) * 512 + (lo * 4 + lax.div(plane, 2)) * 64
+            assemble(src, (role * 4 + j) * 2 + lo, right_m, pl.multiple_of(at, 64))
+
+    def direct(j, _):
+        assemble_right(recv_r, 0, j, lax.rem(z + 8 - j, 8))
+        assemble_right(recv_r, 1, j, lax.rem(z + j, 8))
+        return 0
+
+    def indirect(j, _):
+        assemble_right(passed, 0, j, lax.rem(z + 1 + j, 8))
+        assemble_right(passed, 1, j, lax.rem(z + 7 - j, 8))
+        return 0
+
+    lax.fori_loop(0, 4, direct, 0)
+    for role in range(2):
+        ref = passed.at[pl.ds(role * 64, 64)]
+        pltpu.make_async_copy(ref, ref, pass_recv_sem.at[role]).wait()
+    lax.fori_loop(0, 4, indirect, 0)
+
+    def part_copy(t, role):
         return pltpu.make_async_remote_copy(
-            recv_r.at[pl.ds((role * 4 + j) * 16, 16)], passed.at[pl.ds(((1 - role) * 4 + j) * 16, 16)],
-            pass_send_sem.at[role, j], pass_recv_sem.at[1 - role, j],
-            device_id=line("z", 7 if role else 1), device_id_type=MESH,
+            part_out.at[t, role], part_in.at[t, role], part_send_sem.at[t, role], part_recv_sem.at[t, role],
+            device_id=sibling, device_id_type=MESH,
         )
 
-    def passed_here(role, j):
-        ref = passed.at[pl.ds((role * 4 + j) * 16, 16)]
-        return pltpu.make_async_copy(ref, ref, pass_recv_sem.at[role, j])
-
-    def part_copy(t, m):
-        columns = pl.ds(0, 256 if 0 < t < 4 else 128)
-        return pltpu.make_async_remote_copy(
-            part_out.at[t // 2, m, :, columns], part_in.at[t // 2, m, :, columns],
-            part_send_sem.at[t // 2, m], part_recv_sem.at[t // 2, m], device_id=sibling, device_id_type=MESH,
-        )
+    def product(role, half):
+        rhs = right_m[pl.ds(pl.multiple_of(role * 1024 + half * 512, 512), 512), :]
+        return lax.dot_general(left_m[role * 128 : role * 128 + 128], rhs, NT, preferred_element_type=F32)
 
     def multiply(t):
-        if t < 4:
-            some = pl.ds(0, 32 if t else 30)
-            pltpu.make_async_copy(recv_r.at[some], recv_r.at[some], recv_r_sem.at[t]).wait()
+        some = pl.ds(0, 32 if t else 30)
+        pltpu.make_async_copy(recv_l.at[some], recv_l.at[some], recv_l_sem.at[t]).wait()
+        for role in range(2):
+            for lo in range(2):
+                assemble(recv_l, (role * 4 + t) * 2 + lo, left_m, role * 128 + lo * 64)
+        for role in range(2):
+            part_out[t, role] = product(role, 1 - core).astype(BF16)
+            part_copy(t, role).start()
+        for role in range(2):
+            acc[role] = product(role, core)
+        for role in range(2):
+            part_copy(t, role).wait_recv()
+            tri = (acc[role] + part_in[t, role].astype(F32)).astype(BF16)
+            for lo in range(2):
+                for kb in range(8):
+                    low = tri[lo * 64 : lo * 64 + 32, kb * 64 : kb * 64 + 64]
+                    high = tri[lo * 64 + 32 : lo * 64 + 64, kb * 64 : kb * 64 + 64]
+                    send2[((role * 4 + t) * 2 + lo) * 8 + kb] = jnp.concatenate([low, high], axis=1)
+
+        def give_back(step, half):
+            part = slice(half * 16, half * 16 + 16)
+            kb = lax.rem(col * 2 + x_hi + step, 8)
+            y_to = lax.div(kb, 2)
+            ka_to = lax.rem(kb, 2) * 2 + core
             for role in range(2):
-                pass_copy(role, t).start()
-        if t > 0:
-            for role in range(2):
-                passed_here(role, t - 1).wait()
-        planes = [z_at[8 - t], z_at[t]] if 0 < t < 4 else [z_at[t]]
-        blocks = 2 * len(planes)
-        width = 64 * blocks
-        kbs = [(n % 2) * 4 + lax.div(planes[n // 2], 2) for n in range(blocks)]
-        homes = [(lax.div(kb, 2), lax.rem(kb, 2) * 2 + core) for kb in kbs]
-        for role in range(2):
-            for n in range(blocks):
-                direct = t == 0 or (t < 4 and n // 2 == role)
-                src, j = (recv_r, t) if direct else (passed, t - 1)
-                assemble(src, (role * 4 + j) * 2 + n % 2, right_m, role * 256 + n * 64)
-
-        def product(m):
-            lhs = left_m[pl.ds(pl.multiple_of(m * 256, 256), 256), :]
-            rhs = right_m[pl.ds(pl.multiple_of(lax.div(m, 2) * 256, 256), width), :]
-            return lax.dot_general(lhs, rhs, NT, preferred_element_type=F32)
-
-        own = lax.rem(z + t, 2) == core
-
-        @pl.when(jnp.logical_not(own))
-        def _():
-            def for_sibling(m, _):
-                part_out[t // 2, m, :, :width] = product(m).astype(BF16)
-                part_copy(t, m).start()
-                return 0
-
-            lax.fori_loop(0, 4, for_sibling, 0)
-
-        @pl.when(own)
-        def _():
-            def for_us(m, _):
-                acc[m, :, :width] = product(m)
-                return 0
-
-            lax.fori_loop(0, 4, for_us, 0)
-
-            def tiles(m, _):
-                part_copy(t, m).wait_recv()
-                tri = (acc[m, :, :width] + part_in[t // 2, m, :, :width].astype(F32)).astype(BF16)
-                for b in range(4):
-                    for n in range(blocks):
-                        low = tri[b * 64 : b * 64 + 32, n * 64 : n * 64 + 64]
-                        high = tri[b * 64 + 32 : b * 64 + 64, n * 64 : n * 64 + 64]
-                        send2[(m * 4 + b) * 8 + kbs[n]] = jnp.concatenate([low, high], axis=1)
-                return 0
-
-            lax.fori_loop(0, 4, tiles, 0)
-
-            def give_back(j, half, here):
-                part = slice(half * 16, half * 16 + 16)
-                for n in range(blocks):
-                    for role, tz in ((0, lax.rem(z + 8 - j, 8)), (1, lax.rem(z + j, 8))):
-                        for lo in range(2):
-                            tile = ((role * 4 + j) * 2 + lo) * 8 + kbs[n]
-                            copy = pltpu.make_async_remote_copy(
-                                send2.at[tile, part], recv2.at[mine[role], part], send2_sem, recv2_sem.at[half],
-                                device_id=(lo * 8 + tz, *homes[n]), device_id_type=MESH,
-                            )
-                            if not here:
-                                copy.start()
-                                continue
-                            ours = (kbs[n] * ROWS + lo * 8 + z) == me
-
-                            @pl.when(ours)
-                            def _():
-                                recv2[mine[role], part] = send2[tile, part]
-
-                            @pl.when(jnp.logical_not(ours))
-                            def _():
-                                copy.start()
-
-                return 0
-
-            for half in range(2):
-                lax.fori_loop(1, 4, lambda j, _: give_back(j, half, False), 0)
-                give_back(0, half, True)
-
-    for t in range(5):
+                for lo in range(2):
+                    tile = ((role * 4 + t) * 2 + lo) * 8 + kb
+                    row_to = lo * 8 + z_at[t if role else (8 - t) % 8]
+                    copy = pltpu.make_async_remote_copy(
+                        send2.at[tile, part], recv2.at[mine[role], part], send2_sem, recv2_sem.at[half],
+                        device_id=(row_to, y_to, ka_to), device_id_type=MESH,
+                    )
+                    if t:
+                        copy.start()
+                        continue
+                    ours = kb * ROWS + row_to == me
+
+                    @pl.when(ours)
+                    def _():
+                        recv2[mine[role], part] = send2[tile, part]
+
+                    @pl.when(jnp.logical_not(ours))
+                    def _():
+                        copy.start()
+
+            return 0
+
+        for half in range(2):
+            lax.fori_loop(0, 8, lambda step, _: give_back(step, half), 0)
+
+    for t in (3, 2, 1, 0):
         multiply(t)
 
     def widen(half):
@@ -351,15 +334,9 @@
     pltpu.make_async_copy(send_r.at[others], send_r.at[others], send_r_sem).wait()
     pltpu.make_async_copy(send2.at[others], send2.at[others], send2_sem).wait()
     for role in range(2):
-        for j in range(4):
-            pass_copy(role, j).wait_send()
-    for t in range(5):
-
-        @pl.when(lax.rem(z + t, 2) != core)
-        def _():
-            for m in range(4):
-                part_copy(t, m).wait_send()
-
+        pass_copy(role).wait_send()
+        for t in range(4):
+            part_copy(t, role).wait_send()
     for c in range(4):
         for copy in quarter(out, out_hbm, out_sem, c):
             copy.wait()
@@ -386,13 +363,13 @@
             pltpu.VMEM((32 * 256, 128), F32),
             pltpu.VMEM((16, 128, 256), BF16),
             *[pltpu.VMEM((CHIPS, 32, 128), BF16)] * 5,
-            pltpu.VMEM((1024, 512), BF16),
-            pltpu.VMEM((512, 512), BF16),
-            pltpu.VMEM((4, 256, 256), F32),
-            *[pltpu.VMEM((3, 4, 256, 256), BF16)] * 2,
+            pltpu.VMEM((256, 512), BF16),
+            pltpu.VMEM((2048, 512), BF16),
+            pltpu.VMEM((2, 128, 512), F32),
+            *[pltpu.VMEM((4, 2, 128, 512), BF16)] * 2,
             *[pltpu.VMEM((CHIPS, 32, 128), BF16)] * 2,
             pltpu.VMEM((16, 128, 256), F32),
-            dma, dma, dma, dma((4,)), dma((2, 4)), dma((2, 4)), dma((3, 4)), dma((3, 4)), dma, dma((2,)),
+            dma, dma((4,)), dma, dma, dma((2,)), dma((2,)), dma((4, 2)), dma((4, 2)), dma, dma((2,)),
         ],
         compiler_params=pltpu.CompilerParams(
             collective_id=0, has_side_effects=True, vmem_limit_bytes=56 * 2**20

time: 84.7 us -> 82 us (0.968)
  the two profiles are of different devices: /device:TPU:1 before, /device:TPU:6 now
where the time goes in v5:
time: 82 us; the launch traced here: 81.2 us
  Pallas kernels  79 us (96%)
  local copies, waits for them, and re-layouts  2.26 us (3%)
    pallas_call x1, Pallas kernels, on_device(): pl.pallas_call(kernel, out_shape=jax.ShapeDtypeStruct((64, 64, 128), BF16...  79 us
    unnamed x1, local copies, waits for them, and re-layouts  2.26 us

profile of v5, /device:TPU:6, one launch (start us, length us, event | category | flops | bytes accessed | tf_op | source)
XLA Modules:
  0.0 81.2 jit_solution(15892187280775506693)
XLA Ops:
  0.0 79.0 %shard_map.109 = bf16[64,64,128]{2,1,0:T(8,128)(2,1)} custom-call(bf16[64,64,128]{2,1,0:T(8,128)(2,1)} %pair_hbm.1, f32[1,128]{1,0:T(1,128)} %bitcast.8, f32[1,128]{1,0:T(1,128)} %bitcast.9, bf16[128,512]{1,0:T(8,128)(2,1)} %refs_2_.1, f32[1,512]{1,0:T(1,128)} %bitcast.7, bf16[128,128]{1,0:T(8,128)(2,1)} %refs_4_.1, f32[1,128]{1,0:T(1,128)} %bitcast.10, ...), custom_call_target="tpu_custom_call" | custom-call | tf_op jit(solution)/shard_map/pallas_call | solution.py:349
  79.0 2.3 %copy.13 = bf16[64,64,128]{2,1,0:T(8,128)(2,1)} copy(bf16[64,64,128]{2,1,0:T(8,128)(2,1)} %shard_map.109) | data formatting | bytes 2097152

commit v6 on v5

--- a/solution.py
+++ b/solution.py
@@ -184,7 +184,7 @@
     for role in range(2):
         recv_l[role * 64 + place] = channel(0, mine[role])
         recv_r[role * 64 + place] = channel(128, mine[role])
-    send_left(3)
+    send_left(2)
 
     def pass_copy(role):
         return pltpu.make_async_remote_copy(
@@ -197,7 +197,7 @@
     pltpu.make_async_copy(recv_r.at[others], recv_r.at[others], recv_r_sem).wait()
     for role in range(2):
         pass_copy(role).start()
-    for j in (2, 1, 0):
+    for j in (3, 1, 0):
         send_left(j)
 
     def gates(r, _):
@@ -296,7 +296,7 @@
         for half in range(2):
             lax.fori_loop(0, 8, lambda step, _: give_back(step, half), 0)
 
-    for t in (3, 2, 1, 0):
+    for t in (2, 3, 1, 0):
         multiply(t)
 
     def widen(half):
@@ -324,7 +324,7 @@
     for half in range(2):
         rows_in = recv2.at[others, pl.ds(half * 16, 16)]
         pltpu.make_async_copy(rows_in, rows_in, recv2_sem.at[half]).wait()
-        lax.fori_loop(0, CHIPS, widen(half), 0, unroll=4)
+        lax.fori_loop(0, CHIPS, widen(half), 0, unroll=16)
         for c in (2 * half, 2 * half + 1):
             lax.fori_loop(4 * c, 4 * c + 4, finish, 0, unroll=4)
             for copy in quarter(out, out_hbm, out_sem, c):

time: 82 us -> 81.9 us (level)
  no operation moved by 1% of the time
where the time goes in v6:
time: 81.9 us; the launch traced here: 80.9 us
  Pallas kernels  78.6 us (96%)
  local copies, waits for them, and re-layouts  2.26 us (3%)
    pallas_call x1, Pallas kernels, on_device(): pl.pallas_call(kernel, out_shape=jax.ShapeDtypeStruct((64, 64, 128), BF16...  78.6 us
    unnamed x1, local copies, waits for them, and re-layouts  2.26 us

profile of v6, /device:TPU:6, one launch (start us, length us, event | category | flops | bytes accessed | tf_op | source)
XLA Modules:
  0.0 80.9 jit_solution(3349024076344359112)
XLA Ops:
  0.0 78.6 %shard_map.109 = bf16[64,64,128]{2,1,0:T(8,128)(2,1)} custom-call(bf16[64,64,128]{2,1,0:T(8,128)(2,1)} %pair_hbm.1, f32[1,128]{1,0:T(1,128)} %bitcast.8, f32[1,128]{1,0:T(1,128)} %bitcast.9, bf16[128,512]{1,0:T(8,128)(2,1)} %refs_2_.1, f32[1,512]{1,0:T(1,128)} %bitcast.7, bf16[128,128]{1,0:T(8,128)(2,1)} %refs_4_.1, f32[1,128]{1,0:T(1,128)} %bitcast.10, ...), custom_call_target="tpu_custom_call" | custom-call | tf_op jit(solution)/shard_map/pallas_call | solution.py:349
  78.6 2.3 %copy.13 = bf16[64,64,128]{2,1,0:T(8,128)(2,1)} copy(bf16[64,64,128]{2,1,0:T(8,128)(2,1)} %shard_map.109) | data formatting | bytes 2097152
